TPU v7x, 32 devices: a whole 2x2x4 slice. The times are simulated.
32 devices in a mesh: img: 4 (over z), gx: 2 (over x), gz: 4 (over y, core).
Axes of the slice: x: 2, y: 2, z: 4, core: 2. Of those that a mesh axis runs over, the one named last changes fastest.
Arguments:
- species: float32 [4, 2, 32, 16, 512], P('img', None, 'gx', None, 'gz'), may hold values from -2.5 to 2.5
- diffusion: float32 [2, 32, 16, 512], P(None, 'gx', None, 'gz'), may hold values from 0.1 to 2
- z_inverse: float32 [2, 512, 512], replicated, may hold values from -1 to 1.5
- starts: int32 [4], replicated, may hold values from -1 to 1, as said below
- weights: float32 [4, 4], replicated, may hold values from -0.1 to 1, as said below
Outputs:
- new_string: float32 [4, 2, 32, 16, 512], P('img', None, 'gx', None, 'gz')
Inputs may be any that keep to these rules, and one draw needn't show every extreme that they name: starts[t] is t - 2 or t - 1. Each row holds the cubic Lagrange weights at a point between the second and third of four equally spaced images.
All inputs are finite; a program needn't handle non-finite values.
Results may differ from a plain program's by a relative error of at most 0.00012.
Values sent between devices are 32-bit elements; how exact they have to be, the bound alone decides.
A program may use at most 64 MiB of HBM per device.

v0:
```python
import jax
import jax.numpy as jnp
from jax import lax
from jax.sharding import PartitionSpec as P

STEPS = 4


step_size = 0.05


def with_halo(cells, sides, width):
    for axis, dim in sides:
        count = lax.axis_size(axis)
        ends = count - 1
        head = lax.slice_in_dim(cells, 0, width, axis=dim)
        tail = lax.slice_in_dim(cells, cells.shape[dim] - width, cells.shape[dim], axis=dim)
        cells = jnp.concatenate(
            [
                lax.ppermute(tail, axis, [(i, (i + 1) % count) for i in range(ends)]),
                cells,
                lax.ppermute(head, axis, [((i + 1) % count, i) for i in range(ends)]),
            ],
            axis=dim,
        )
    return cells


def passed_along(value, axis, steps):
    count = lax.axis_size(axis)
    first, last = (max(0, -steps), min(count, count - steps))
    return lax.ppermute(value, axis, [(source, source + steps) for source in range(first, last)])


def reaction(state):
    first = state[0]
    second = state[1]
    return jnp.stack([first - first * first * first - second + 0.2, 0.5 * (first - second)])


def spread_flux(state, padded, coeffs):
    centre = coeffs[:, 1:-1, 1:-1]
    total = (centre + coeffs[:, :-2, 1:-1]) * (padded[:, :-2, 1:-1] - state)
    total = total + (centre + coeffs[:, 2:, 1:-1]) * (padded[:, 2:, 1:-1] - state)
    total = total + (centre + coeffs[:, 1:-1, :-2]) * (padded[:, 1:-1, :-2] - state)
    total = total + (centre + coeffs[:, 1:-1, 2:]) * (padded[:, 1:-1, 2:] - state)
    return 0.5 * total


def local(species, diffusion, z_inverse, starts, weights):
    state = species[0]
    y_widths = ((0, 0), (0, 0), (1, 1), (0, 0))
    coeffs = with_halo(diffusion, (("gx", 1),), 1)
    coeffs = jnp.pad(coeffs, y_widths)
    for repeat in range(STEPS):
        padded = with_halo(state, (("gx", 1),), 1)
        padded = jnp.pad(padded, y_widths)
        source = state + step_size * (reaction(state) + spread_flux(state, padded, coeffs))
        solved = jnp.einsum(
            "sij,sabj->sabi",
            z_inverse,
            lax.all_to_all(source, "gz", split_axis=2, concat_axis=3, tiled=True),
            precision=lax.Precision.HIGHEST,
        )
        state = lax.all_to_all(solved, "gz", split_axis=3, concat_axis=2, tiled=True)
    before_one = passed_along(state, "img", 1)
    before_two = passed_along(state, "img", 2)
    after_one = passed_along(state, "img", -1)
    after_two = passed_along(state, "img", -2)
    images = lax.axis_size("img")
    target = lax.axis_index("img")
    listed = jnp.arange(images, dtype=jnp.int32)
    picked = listed == target
    first_image = jnp.sum(jnp.where(picked, starts, 0))
    my_weights = jnp.sum(jnp.where(picked[:, None], weights, 0.0), axis=0)
    sources = {-2: before_two, -1: before_one, 0: state, 1: after_one, 2: after_two}
    result = None
    for offset in range(-2, 3):
        coef = jnp.zeros((), jnp.float32)
        for place in range(4):
            coef = coef + jnp.where(first_image + place == target + offset, my_weights[place], 0.0)
        term = coef * sources[offset]
        result = term if result is None else result + term
    return result[None]


def solution(mesh):
    return jax.shard_map(
        local,
        mesh=mesh,
        in_specs=(P("img", None, "gx", None, "gz"), P(None, "gx", None, "gz"), P(), P(), P()),
        out_specs=P("img", None, "gx", None, "gz"),
        check_vma=False,
    )
```

profile of v0, /device:TPU:0, one launch (start us, length us, event | category | flops | bytes accessed | tf_op | source)
XLA Modules:
  0.0 200.6 jit_solution(16023715058296012637)
XLA Ops:
  0.9 4.8 %collective-permute-start = (f32[2,1,16,128]{3,1,0,2:T(1,128)S(1)}, f32[2,1,16,128]{3,1,0,2:T(1,128)S(1)}, u32[]{:S(2)}, u32[]{:S(2)}) collective-permute-start(f32[2,1,16,128]{3,1,0,2:T(1,128)S(1)} %copy.23), channel_id=1, source_target_pairs={{0,4},{1,5},{2,6},{3,7},{8,12},{9,13},{10,14},{11,15},{16,20},{17,... | collective-permute-start | bytes 49160 | tf_op jit(solution)/shard_map/ppermute | solution.py:20
  8.2 4.5 %collective-permute-start.1 = (f32[2,1,16,128]{3,1,0,2:T(1,128)S(1)}, f32[2,1,16,128]{3,1,0,2:T(1,128)S(1)}, u32[]{:S(2)}, u32[]{:S(2)}) collective-permute-start(f32[2,1,16,128]{3,1,0,2:T(1,128)S(1)} %get-tuple-element.32), channel_id=1, source_target_pairs={{0,4},{1,5},{2,6},{3,7},{8,12},{9,13},{10,14},{11,15},{16,20},{17,... | collective-permute-start | bytes 49160 | tf_op jit(solution)/shard_map/ppermute | solution.py:20
  18.9 8.6 %all_to_all.144 = f32[2,16,16,128]{3,1,0,2:T(8,128)S(1)} all-to-all(f32[2,16,16,128]{3,1,0,2:T(8,128)S(1)} %get-tuple-element.5), channel_id=1, replica_groups=mesh['img'=4,'gx'=2,'gz'=4] {'gz'}, dimensions={2} | all-to-all | bytes 524288 | tf_op jit(solution)/shard_map/all_to_all | solution.py:62
  33.4 3.1 %reshape.265 = f32[4,1,16384]{2,1,0:T(1,128)S(1)} reshape(f32[512,2,4,16]{3,2,1,0:T(4,128)} %bitcast.108) | data formatting | bytes 524288
  36.4 8.4 %all_to_all.145 = f32[4,1,16384]{2,1,0:T(1,128)S(1)} all-to-all(f32[4,1,16384]{2,1,0:T(1,128)S(1)} %reshape.265), channel_id=1, replica_groups=mesh['img'=4,'gx'=2,'gz'=4] {'gz'}, dimensions={0} | all-to-all | bytes 524288 | tf_op jit(solution)/shard_map/all_to_all | solution.py:65
  46.9 2.9 %reshape.266 = f32[512,2,4,16]{3,2,1,0:T(4,128)} reshape(f32[4,16384]{1,0:T(4,128)S(1)} %reduce) | data formatting | bytes 524288
  55.4 4.2 %collective-permute-done.5 = f32[2,1,16,128]{3,1,0,2:T(1,128)S(1)} collective-permute-done((f32[2,1,16,128]{3,1,0,2:T(1,128)S(1)}, f32[2,1,16,128]{3,1,0,2:T(1,128)S(1)}, u32[]{:S(2)}, u32[]{:S(2)}) %collective-permute-start.5) | collective-permute-done | bytes 16416 | tf_op jit(solution)/shard_map/ppermute | solution.py:22
  60.0 8.4 %all_to_all.146 = f32[2,16,16,128]{3,1,0,2:T(8,128)S(1)} all-to-all(f32[2,16,16,128]{3,1,0,2:T(8,128)S(1)} %fusion.40), channel_id=1, replica_groups=mesh['img'=4,'gx'=2,'gz'=4] {'gz'}, dimensions={2} | all-to-all | bytes 524288 | tf_op jit(solution)/shard_map/all_to_all | solution.py:62
  74.2 3.1 %reshape.267 = f32[4,1,16384]{2,1,0:T(1,128)S(1)} reshape(f32[512,2,4,16]{3,2,1,0:T(4,128)} %bitcast.110) | data formatting | bytes 524288
  77.3 8.4 %all_to_all.147 = f32[4,1,16384]{2,1,0:T(1,128)S(1)} all-to-all(f32[4,1,16384]{2,1,0:T(1,128)S(1)} %reshape.267), channel_id=1, replica_groups=mesh['img'=4,'gx'=2,'gz'=4] {'gz'}, dimensions={0} | all-to-all | bytes 524288 | tf_op jit(solution)/shard_map/all_to_all | solution.py:65
  87.1 2.9 %reshape.268 = f32[512,2,4,16]{3,2,1,0:T(4,128)} reshape(f32[4,16384]{1,0:T(4,128)S(1)} %reduce.1) | data formatting | bytes 524288
  94.9 4.2 %collective-permute-done.7 = f32[2,1,16,128]{3,1,0,2:T(1,128)S(1)} collective-permute-done((f32[2,1,16,128]{3,1,0,2:T(1,128)S(1)}, f32[2,1,16,128]{3,1,0,2:T(1,128)S(1)}, u32[]{:S(2)}, u32[]{:S(2)}) %collective-permute-start.7) | collective-permute-done | bytes 16416 | tf_op jit(solution)/shard_map/ppermute | solution.py:22
  99.5 8.4 %all_to_all.148 = f32[2,16,16,128]{3,1,0,2:T(8,128)S(1)} all-to-all(f32[2,16,16,128]{3,1,0,2:T(8,128)S(1)} %fusion.27), channel_id=1, replica_groups=mesh['img'=4,'gx'=2,'gz'=4] {'gz'}, dimensions={2} | all-to-all | bytes 524288 | tf_op jit(solution)/shard_map/all_to_all | solution.py:62
  113.8 3.1 %reshape.269 = f32[4,1,16384]{2,1,0:T(1,128)S(1)} reshape(f32[512,2,4,16]{3,2,1,0:T(4,128)} %bitcast.112) | data formatting | bytes 524288
  116.8 8.4 %all_to_all.149 = f32[4,1,16384]{2,1,0:T(1,128)S(1)} all-to-all(f32[4,1,16384]{2,1,0:T(1,128)S(1)} %reshape.269), channel_id=1, replica_groups=mesh['img'=4,'gx'=2,'gz'=4] {'gz'}, dimensions={0} | all-to-all | bytes 524288 | tf_op jit(solution)/shard_map/all_to_all | solution.py:65
  126.7 2.9 %reshape.270 = f32[512,2,4,16]{3,2,1,0:T(4,128)} reshape(f32[4,16384]{1,0:T(4,128)S(1)} %reduce.2) | data formatting | bytes 524288
  134.5 4.2 %collective-permute-done.9 = f32[2,1,16,128]{3,1,0,2:T(1,128)S(1)} collective-permute-done((f32[2,1,16,128]{3,1,0,2:T(1,128)S(1)}, f32[2,1,16,128]{3,1,0,2:T(1,128)S(1)}, u32[]{:S(2)}, u32[]{:S(2)}) %collective-permute-start.9) | collective-permute-done | bytes 16416 | tf_op jit(solution)/shard_map/ppermute | solution.py:22
  139.1 8.4 %all_to_all.150 = f32[2,16,16,128]{3,1,0,2:T(8,128)S(1)} all-to-all(f32[2,16,16,128]{3,1,0,2:T(8,128)S(1)} %fusion.14), channel_id=1, replica_groups=mesh['img'=4,'gx'=2,'gz'=4] {'gz'}, dimensions={2} | all-to-all | bytes 524288 | tf_op jit(solution)/shard_map/all_to_all | solution.py:62
  151.7 3.7 %reshape.271 = f32[4,1,16384]{2,1,0:T(1,128)} reshape(f32[512,2,4,16]{3,2,1,0:T(4,128)} %bitcast.114) | data formatting | bytes 524288
  155.4 3.4 %all-to-all-start.7 = ((f32[4,1,16384]{2,1,0:T(1,128)}), f32[4,1,16384]{2,1,0:T(1,128)S(1)}, u32[]{:S(2)}, u32[]{:S(2)}) async-start(f32[4,1,16384]{2,1,0:T(1,128)} %reshape.271), calls=%async_computation.7 | async-start | bytes 524288 | tf_op jit(solution)/shard_map/all_to_all | solution.py:65
  159.4 5.4 %all-to-all-done.7 = f32[4,1,16384]{2,1,0:T(1,128)S(1)} async-done(((f32[4,1,16384]{2,1,0:T(1,128)}), f32[4,1,16384]{2,1,0:T(1,128)S(1)}, u32[]{:S(2)}, u32[]{:S(2)}) %all-to-all-start.7) | async-done | bytes 262176 | tf_op jit(solution)/shard_map/all_to_all | solution.py:65
  166.2 2.9 %reshape.272 = f32[512,2,4,16]{3,2,1,0:T(4,128)} reshape(f32[4,16384]{1,0:T(4,128)S(1)} %reduce.3) | data formatting | bytes 524288
  171.0 4.5 %collective-permute-start.10 = (f32[2,16,16,128]{3,2,1,0:T(8,128)S(1)}, f32[2,16,16,128]{3,2,1,0:T(8,128)S(1)}, u32[]{:S(2)}, u32[]{:S(2)}) collective-permute-start(f32[2,16,16,128]{3,2,1,0:T(8,128)S(1)} %bitcast.131), channel_id=1, source_target_pairs={{0,16},{8,24},{1,17},{9,25},{2,18},{10,26},{3,19},{11,27},{4,20},{... | collective-permute-start | bytes 786440 | tf_op jit(solution)/shard_map/ppermute | solution.py:32
  175.5 3.5 %collective-permute-start.11 = (f32[2,16,16,128]{3,2,1,0:T(8,128)S(1)}, f32[2,16,16,128]{3,2,1,0:T(8,128)S(1)}, u32[]{:S(2)}, u32[]{:S(2)}) collective-permute-start(f32[2,16,16,128]{3,2,1,0:T(8,128)S(1)} %bitcast.132), channel_id=1, source_target_pairs={{0,8},{8,16},{16,24},{1,9},{9,17},{17,25},{2,10},{10,18},{18,26},{... | collective-permute-start | bytes 786440 | tf_op jit(solution)/shard_map/ppermute | solution.py:32
  (85 shorter events, 60.5 us)
Async XLA Ops:
  0.0 29.5 %copy-start = (f32[2,512,512]{2,1,0:T(8,128)S(1)}, f32[2,512,512]{2,1,0:T(8,128)}, u32[]{:S(2)}) copy-start(f32[2,512,512]{2,1,0:T(8,128)} %param.7) | copy-start | bytes 6291460
  0.0 18.5 %copy-start.1 = (f32[2,16,16,128]{3,2,1,0:T(8,128)S(1)}, f32[2,16,16,128]{3,2,1,0:T(8,128)}, u32[]{:S(2)}) copy-start(f32[2,16,16,128]{3,2,1,0:T(8,128)} %param.6) | copy-start | bytes 786436
  0.9 17.5 %collective-permute-start = (f32[2,1,16,128]{3,1,0,2:T(1,128)S(1)}, f32[2,1,16,128]{3,1,0,2:T(1,128)S(1)}, u32[]{:S(2)}, u32[]{:S(2)}) collective-permute-start(f32[2,1,16,128]{3,1,0,2:T(1,128)S(1)} %copy.23), channel_id=1, source_target_pairs={{0,4},{1,5},{2,6},{3,7},{8,12},{9,13},{10,14},{11,15},{16,20},{17,... | collective-permute-start | bytes 49160 | tf_op jit(solution)/shard_map/ppermute | solution.py:20
  5.8 12.6 %collective-permute-start.2 = (f32[2,1,16,128]{3,1,0,2:T(1,128)S(1)}, f32[2,1,16,128]{3,1,0,2:T(1,128)S(1)}, u32[]{:S(2)}, u32[]{:S(2)}) collective-permute-start(f32[2,1,16,128]{3,1,0,2:T(1,128)S(1)} %copy.26), channel_id=1, source_target_pairs={{4,0},{5,1},{6,2},{7,3},{12,8},{13,9},{14,10},{15,11},{20,16},{21,... | collective-permute-start | bytes 49160 | tf_op jit(solution)/shard_map/ppermute | solution.py:22
  8.2 8.0 %collective-permute-start.1 = (f32[2,1,16,128]{3,1,0,2:T(1,128)S(1)}, f32[2,1,16,128]{3,1,0,2:T(1,128)S(1)}, u32[]{:S(2)}, u32[]{:S(2)}) collective-permute-start(f32[2,1,16,128]{3,1,0,2:T(1,128)S(1)} %get-tuple-element.32), channel_id=1, source_target_pairs={{0,4},{1,5},{2,6},{3,7},{8,12},{9,13},{10,14},{11,15},{16,20},{17,... | collective-permute-start | bytes 49160 | tf_op jit(solution)/shard_map/ppermute | solution.py:20
  12.7 5.6 %collective-permute-start.3 = (f32[2,1,16,128]{3,1,0,2:T(1,128)S(1)}, f32[2,1,16,128]{3,1,0,2:T(1,128)S(1)}, u32[]{:S(2)}, u32[]{:S(2)}) collective-permute-start(f32[2,1,16,128]{3,1,0,2:T(1,128)S(1)} %get-tuple-element.33), channel_id=1, source_target_pairs={{4,0},{5,1},{6,2},{7,3},{12,8},{13,9},{14,10},{15,11},{20,16},{21,... | collective-permute-start | bytes 49160 | tf_op jit(solution)/shard_map/ppermute | solution.py:22
  51.6 3.8 %collective-permute-start.4 = (f32[2,1,16,128]{3,1,0,2:T(1,128)S(1)}, f32[2,1,16,128]{3,1,0,2:T(1,128)S(1)}, u32[]{:S(2)}, u32[]{:S(2)}) collective-permute-start(f32[2,1,16,128]{3,1,0,2:T(1,128)S(1)} %get-tuple-element.24), channel_id=1, source_target_pairs={{0,4},{1,5},{2,6},{3,7},{8,12},{9,13},{10,14},{11,15},{16,20},{17,... | collective-permute-start | bytes 49160 | tf_op jit(solution)/shard_map/ppermute | solution.py:20
  54.0 5.6 %collective-permute-start.5 = (f32[2,1,16,128]{3,1,0,2:T(1,128)S(1)}, f32[2,1,16,128]{3,1,0,2:T(1,128)S(1)}, u32[]{:S(2)}, u32[]{:S(2)}) collective-permute-start(f32[2,1,16,128]{3,1,0,2:T(1,128)S(1)} %get-tuple-element.25), channel_id=1, source_target_pairs={{4,0},{5,1},{6,2},{7,3},{12,8},{13,9},{14,10},{15,11},{20,16},{21,... | collective-permute-start | bytes 49160 | tf_op jit(solution)/shard_map/ppermute | solution.py:22
  91.9 3.1 %collective-permute-start.6 = (f32[2,1,16,128]{3,1,0,2:T(1,128)S(1)}, f32[2,1,16,128]{3,1,0,2:T(1,128)S(1)}, u32[]{:S(2)}, u32[]{:S(2)}) collective-permute-start(f32[2,1,16,128]{3,1,0,2:T(1,128)S(1)} %get-tuple-element.18), channel_id=1, source_target_pairs={{0,4},{1,5},{2,6},{3,7},{8,12},{9,13},{10,14},{11,15},{16,20},{17,... | collective-permute-start | bytes 49160 | tf_op jit(solution)/shard_map/ppermute | solution.py:20
  93.5 5.6 %collective-permute-start.7 = (f32[2,1,16,128]{3,1,0,2:T(1,128)S(1)}, f32[2,1,16,128]{3,1,0,2:T(1,128)S(1)}, u32[]{:S(2)}, u32[]{:S(2)}) collective-permute-start(f32[2,1,16,128]{3,1,0,2:T(1,128)S(1)} %get-tuple-element.19), channel_id=1, source_target_pairs={{4,0},{5,1},{6,2},{7,3},{12,8},{13,9},{14,10},{15,11},{20,16},{21,... | collective-permute-start | bytes 49160 | tf_op jit(solution)/shard_map/ppermute | solution.py:22
  131.4 3.1 %collective-permute-start.8 = (f32[2,1,16,128]{3,1,0,2:T(1,128)S(1)}, f32[2,1,16,128]{3,1,0,2:T(1,128)S(1)}, u32[]{:S(2)}, u32[]{:S(2)}) collective-permute-start(f32[2,1,16,128]{3,1,0,2:T(1,128)S(1)} %get-tuple-element.12), channel_id=1, source_target_pairs={{0,4},{1,5},{2,6},{3,7},{8,12},{9,13},{10,14},{11,15},{16,20},{17,... | collective-permute-start | bytes 49160 | tf_op jit(solution)/shard_map/ppermute | solution.py:20
  133.1 5.6 %collective-permute-start.9 = (f32[2,1,16,128]{3,1,0,2:T(1,128)S(1)}, f32[2,1,16,128]{3,1,0,2:T(1,128)S(1)}, u32[]{:S(2)}, u32[]{:S(2)}) collective-permute-start(f32[2,1,16,128]{3,1,0,2:T(1,128)S(1)} %get-tuple-element.13), channel_id=1, source_target_pairs={{4,0},{5,1},{6,2},{7,3},{12,8},{13,9},{14,10},{15,11},{20,16},{21,... | collective-permute-start | bytes 49160 | tf_op jit(solution)/shard_map/ppermute | solution.py:22
  149.9 8.9 %copy-start.3 = (s32[4]{0:T(128)S(1)}, s32[4]{0:T(128)}, u32[]{:S(2)}) copy-start(s32[4]{0:T(128)} %param.8) | copy-start | bytes 52
  155.4 9.4 %all-to-all-start.7 = ((f32[4,1,16384]{2,1,0:T(1,128)}), f32[4,1,16384]{2,1,0:T(1,128)S(1)}, u32[]{:S(2)}, u32[]{:S(2)}) async-start(f32[4,1,16384]{2,1,0:T(1,128)} %reshape.271), calls=%async_computation.7 | async-start | bytes 524288 | tf_op jit(solution)/shard_map/all_to_all | solution.py:65
  166.2 19.9 %copy-start.2 = (f32[4,4]{1,0:T(4,128)S(1)}, f32[4,4]{1,0:T(4,128)}, u32[]{:S(2)}) copy-start(f32[4,4]{1,0:T(4,128)} %param.9) | copy-start | bytes 196
  171.0 28.8 %collective-permute-start.10 = (f32[2,16,16,128]{3,2,1,0:T(8,128)S(1)}, f32[2,16,16,128]{3,2,1,0:T(8,128)S(1)}, u32[]{:S(2)}, u32[]{:S(2)}) collective-permute-start(f32[2,16,16,128]{3,2,1,0:T(8,128)S(1)} %bitcast.131), channel_id=1, source_target_pairs={{0,16},{8,24},{1,17},{9,25},{2,18},{10,26},{3,19},{11,27},{4,20},{... | collective-permute-start | bytes 786440 | tf_op jit(solution)/shard_map/ppermute | solution.py:32
  175.5 24.3 %collective-permute-start.11 = (f32[2,16,16,128]{3,2,1,0:T(8,128)S(1)}, f32[2,16,16,128]{3,2,1,0:T(8,128)S(1)}, u32[]{:S(2)}, u32[]{:S(2)}) collective-permute-start(f32[2,16,16,128]{3,2,1,0:T(8,128)S(1)} %bitcast.132), channel_id=1, source_target_pairs={{0,8},{8,16},{16,24},{1,9},{9,17},{17,25},{2,10},{10,18},{18,26},{... | collective-permute-start | bytes 786440 | tf_op jit(solution)/shard_map/ppermute | solution.py:32
  179.0 20.8 %collective-permute-start.12 = (f32[2,16,16,128]{3,2,1,0:T(8,128)S(1)}, f32[2,16,16,128]{3,2,1,0:T(8,128)S(1)}, u32[]{:S(2)}, u32[]{:S(2)}) collective-permute-start(f32[2,16,16,128]{3,2,1,0:T(8,128)S(1)} %bitcast.133), channel_id=1, source_target_pairs={{8,0},{16,8},{24,16},{9,1},{17,9},{25,17},{10,2},{18,10},{26,18},{... | collective-permute-start | bytes 786440 | tf_op jit(solution)/shard_map/ppermute | solution.py:32
  180.3 19.5 %collective-permute-start.13 = (f32[2,16,16,128]{3,2,1,0:T(8,128)S(1)}, f32[2,16,16,128]{3,2,1,0:T(8,128)S(1)}, u32[]{:S(2)}, u32[]{:S(2)}) collective-permute-start(f32[2,16,16,128]{3,2,1,0:T(8,128)S(1)} %bitcast.134), channel_id=1, source_target_pairs={{16,0},{24,8},{17,1},{25,9},{18,2},{26,10},{19,3},{27,11},{20,4},{... | collective-permute-start | bytes 786440 | tf_op jit(solution)/shard_map/ppermute | solution.py:32
where the time goes:
time: 203 us; the launch traced here: 201 us
  blocking collectives  59.2 us (29%)
  local copies, waits for them, and re-layouts  50.2 us (25%)
  starting transfers between devices  35.5 us (17%)
  waiting for transfers between devices  20.4 us (10%)
  between operations  17.8 us (9%)
  other arithmetic  8.99 us (4%)
  matrix products  8.52 us (4%)
    all_to_all x4, blocking collectives, local(): lax.all_to_all(source, 'gz', split_axis=2, concat_axis=3, tiled=True)  33.9 us
    unnamed x18, local copies, waits for them, and re-layouts  26.4 us
    all_to_all x3, blocking collectives, local(): lax.all_to_all(solved, 'gz', split_axis=3, concat_axis=2, tiled=True)  25.3 us
    ppermute x5, starting transfers between devices, with_halo(): lax.ppermute(tail, axis, [(i, (i + 1) % count) for i in range(ends)])  15 us
    ppermute x5, waiting for transfers between devices, with_halo(): lax.ppermute(head, axis, [((i + 1) % count, i) for i in range(ends)])  14.8 us
    ppermute x4, starting transfers between devices, passed_along(): lax.ppermute(value, axis, [(source, source + steps) for source in range(f...  10.6 us
    dot_general x4, matrix products, local(): jnp.einsum('sij,sabj->sabi', z_inverse, lax.all_to_all(source, 'gz', spli...  8.52 us
    all_to_all x5, local copies, waits for them, and re-layouts, local(): lax.all_to_all(solved, 'gz', split_axis=3, concat_axis=2, tiled=True)  7.99 us
  transfers between devices with their start and end apart: 15, of which 8 were waited for; matrix products, arithmetic and copies ran while one was open for 2% of the time, Pallas kernels for 0%

commit v1 on v0

v1 whole, which is shorter than its diff:
```python
import functools

import jax
import jax.numpy as jnp
from jax import lax
from jax.experimental import pallas as pl
from jax.experimental.pallas import tpu as pltpu
from jax.sharding import PartitionSpec as P

STEPS = 4
HALO = 1


step_size = 0.05
MESH = pl.DeviceIdType.MESH
both = (0, 1)


def kernel(
    sizes,
    species_ref,
    diffusion_ref,
    z_ref,
    starts_ref,
    weights_ref,
    out_ref,
    z_raw,
    z_high,
    z_low,
    coeffs,
    states,
    lhs,
    evolved,
    near,
    far,
    result,
    local_sem,
    swap_send,
    swap_recv,
    edge_send,
    edge_recv,
    row_send,
    row_recv,
    near_send,
    near_recv,
    far_send,
    far_recv,
    back_send,
    back_recv,
):
    images, nx, nz, width, ny, lanes = sizes
    rows = width // nz
    image, gx, gz = lax.axis_index("img"), lax.axis_index("gx"), lax.axis_index("gz")
    strip = gx * nz + gz
    strips = nx * nz
    full = rows + 2 * HALO

    load_z = pltpu.make_async_copy(z_ref, z_raw, local_sem.at[0])
    load_z.start()

    barrier = pltpu.get_barrier_semaphore()
    for step in range(1, nz):
        other = lax.rem(gz + step, nz)
        pl.semaphore_signal(barrier, inc=1, device_id={"gz": other}, device_id_type=MESH)

    def greet(condition, where):
        @pl.when(condition)
        def _():
            pl.semaphore_signal(barrier, inc=1, device_id=where, device_id_type=MESH)

    greet(image > 0, {"img": image - 1})
    greet(image < images - 1, {"img": image + 1})
    greet(gx > 0, {"gx": gx - 1, "gz": nz - 1})
    greet(gx < nx - 1, {"gx": gx + 1, "gz": 0})

    @pl.when(gz == 0)
    def _():
        for other in range(nz):
            greet(gx > 0, {"gx": gx - 1, "gz": other})

    @pl.when(gz == nz - 1)
    def _():
        for other in range(nz):
            greet(gx < nx - 1, {"gx": gx + 1, "gz": other})

    def one(condition):
        return jnp.where(condition, 1, 0)

    below, above = one(gx > 0), one(gx < nx - 1)
    expected = (nz - 1) + one(image > 0) + one(image < images - 1) + below + above
    expected = expected + nz * (below * one(gz == 0) + above * one(gz == nz - 1))
    pl.semaphore_wait(barrier, expected)

    sources = (diffusion_ref, species_ref.at[0])
    targets = (coeffs, states.at[0])

    def span(k):
        return max(0, k * rows - HALO), min(width, k * rows + rows + HALO)

    def swap(which, k, sender):
        low, high = span(k)
        first = low - (k * rows - HALO)
        return pltpu.make_async_remote_copy(
            src_ref=sources[which].at[:, low:high],
            dst_ref=targets[which].at[:, sender, first : first + high - low],
            send_sem=swap_send.at[which, k],
            recv_sem=swap_recv.at[which, sender],
            device_id={"gz": k},
            device_id_type=MESH,
        )

    def own(which, k):
        low, high = span(k)
        first = low - (k * rows - HALO)
        return pltpu.make_async_copy(
            sources[which].at[:, low:high],
            targets[which].at[:, k, first : first + high - low],
            local_sem.at[1 + which],
        )

    def edge_up(which, sender):
        return pltpu.make_async_remote_copy(
            src_ref=sources[which].at[:, width - HALO : width],
            dst_ref=targets[which].at[:, sender, 0:HALO],
            send_sem=edge_send.at[which, 0],
            recv_sem=edge_recv.at[which, 0, sender],
            device_id={"gx": gx + 1, "gz": 0},
            device_id_type=MESH,
        )

    def edge_down(which, sender):
        return pltpu.make_async_remote_copy(
            src_ref=sources[which].at[:, 0:HALO],
            dst_ref=targets[which].at[:, sender, rows + HALO : full],
            send_sem=edge_send.at[which, 1],
            recv_sem=edge_recv.at[which, 1, sender],
            device_id={"gx": gx - 1, "gz": nz - 1},
            device_id_type=MESH,
        )

    for which in (1, 0):
        for me in range(nz):

            @pl.when(gz == me)
            def _(which=which, me=me):
                for step in range(1, nz):
                    swap(which, (me + step) % nz, me).start()
                own(which, me).start()

        @pl.when(gx < nx - 1)
        def _(which=which):
            edge_up(which, gz).start()

        @pl.when(gx > 0)
        def _(which=which):
            edge_down(which, gz).start()

    @pl.when(strip == 0)
    def _():
        for part in (coeffs, *[states.at[i] for i in range(STEPS)]):
            part[:, :, 0:HALO] = jnp.zeros((2, nz, HALO, ny, lanes), jnp.float32)

    @pl.when(strip == strips - 1)
    def _():
        for part in (coeffs, *[states.at[i] for i in range(STEPS)]):
            part[:, :, rows + HALO : full] = jnp.zeros((2, nz, HALO, ny, lanes), jnp.float32)

    def clear(condition, part):
        @pl.when(condition)
        def _():
            part[...] = jnp.zeros(part.shape, jnp.float32)

    clear(image < 1, near.at[0])
    clear(image > images - 2, near.at[1])
    clear(image < 2, far.at[0])
    clear(image > images - 3, far.at[1])

    load_z.wait()
    for s in both:
        for block in range(nz):
            part = slice(block * lanes, (block + 1) * lanes)
            turned = z_raw[s, part, :].T
            high = turned.astype(jnp.bfloat16)
            z_high[s, :, part] = high
            z_low[s, :, part] = (turned - high.astype(jnp.float32)).astype(jnp.bfloat16)

    def arrived(which):
        for me in range(nz):

            @pl.when(gz == me)
            def _(me=me):
                own(which, me).wait()
                for sender in range(nz):
                    if sender != me:
                        low, high = span(me)
                        first = low - (me * rows - HALO)
                        part = targets[which].at[:, sender, first : first + high - low]
                        pltpu.make_async_copy(part, part, swap_recv.at[which, sender]).wait()

        @pl.when((gz == 0) & (gx > 0))
        def _():
            for sender in range(nz):
                edge_up(which, sender).wait_recv()

        @pl.when((gz == nz - 1) & (gx < nx - 1))
        def _():
            for sender in range(nz):
                edge_down(which, sender).wait_recv()

    def row_up(step, s):
        p = strip + 1
        return pltpu.make_async_remote_copy(
            src_ref=states.at[step, s, :, rows],
            dst_ref=states.at[step, s, :, 0],
            send_sem=row_send.at[step, s, 0],
            recv_sem=row_recv.at[step, s, 0],
            device_id={"gx": lax.div(p, nz), "gz": lax.rem(p, nz)},
            device_id_type=MESH,
        )

    def row_down(step, s):
        p = strip - 1 + nz
        return pltpu.make_async_remote_copy(
            src_ref=states.at[step, s, :, 1],
            dst_ref=states.at[step, s, :, rows + 1],
            send_sem=row_send.at[step, s, 1],
            recv_sem=row_recv.at[step, s, 1],
            device_id={"gx": lax.div(p, nz) - 1, "gz": lax.rem(p, nz)},
            device_id_type=MESH,
        )

    place = lax.broadcasted_iota(jnp.int32, (rows, ny, lanes), 1)
    arrived(1)
    arrived(0)
    half = 0.5 * step_size
    cells = rows * ny

    def to_near(s, g, side):
        return pltpu.make_async_remote_copy(
            src_ref=evolved.at[s, g],
            dst_ref=near.at[side, s, g],
            send_sem=near_send.at[side, s, g],
            recv_sem=near_recv.at[side, s, g],
            device_id={"img": image + 1 - 2 * side},
            device_id_type=MESH,
        )

    def to_far(s, g, side):
        return pltpu.make_async_remote_copy(
            src_ref=near.at[side, s, g],
            dst_ref=far.at[side, s, g],
            send_sem=far_send.at[side, s, g],
            recv_sem=far_recv.at[side, s, g],
            device_id={"img": image + 1 - 2 * side},
            device_id_type=MESH,
        )

    can_send = (image < images - 1, image > 0)
    has_near = (image > 0, image < images - 1)
    has_far = (image > 1, image < images - 2)

    for step in range(STEPS):
        state = states.at[step]
        if step > 0:
            for s in both:

                @pl.when(strip > 0)
                def _(s=s):
                    row_up(step, s).wait_recv()

                @pl.when(strip < strips - 1)
                def _(s=s):
                    row_down(step, s).wait_recv()

        for g in range(nz):
            first, second = state[0, g, 1 : rows + 1], state[1, g, 1 : rows + 1]
            reactions = (
                first - first * first * first - second + 0.2,
                0.5 * (first - second),
            )
            for s in both:
                c = state[s, g]
                d = coeffs[s, g]
                across = (d[:-1] + d[1:]) * (c[1:] - c[:-1])
                centre, spread = c[1:-1], d[1:-1]
                last = place == ny - 1
                c_next = jnp.where(last, 0.0, pltpu.roll(centre, ny - 1, 1))
                d_next = jnp.where(last, 0.0, pltpu.roll(spread, ny - 1, 1))
                along = (spread + d_next) * (c_next - centre)
                before = jnp.where(place == 0, spread * centre, pltpu.roll(along, 1, 1))
                flux = (across[1:] - across[:-1]) + (along - before)
                source = centre + step_size * reactions[s] + half * flux
                source = source.reshape(cells, lanes)
                high = source.astype(jnp.bfloat16)
                part = slice(g * lanes, (g + 1) * lanes)
                lhs[s, 0:cells, part] = high
                lhs[s, cells : 2 * cells, part] = (source - high.astype(jnp.float32)).astype(jnp.bfloat16)

        for s in both:
            product = jnp.dot(lhs[s], z_high[s], preferred_element_type=jnp.float32)
            small = jnp.dot(lhs[s, 0:cells], z_low[s], preferred_element_type=jnp.float32)
            solved = product[0:cells] + (product[cells : 2 * cells] + small)
            for g in range(nz):
                block = solved[:, g * lanes : (g + 1) * lanes].reshape(rows, ny, lanes)
                if step < STEPS - 1:
                    states[step + 1, s, g, 1 : rows + 1] = block
                else:
                    evolved[s, g] = block
            if step < STEPS - 1:

                @pl.when(strip < strips - 1)
                def _(s=s, step=step):
                    row_up(step + 1, s).start()

                @pl.when(strip > 0)
                def _(s=s, step=step):
                    row_down(step + 1, s).start()

            else:
                for g in range(nz):
                    for side in both:

                        @pl.when(can_send[side])
                        def _(s=s, g=g, side=side):
                            to_near(s, g, side).start()

    for s in both:
        for g in range(nz):
            for side in both:

                @pl.when(has_near[side])
                def _(s=s, g=g, side=side):
                    to_near(s, g, side).wait_recv()

                    @pl.when(can_send[side])
                    def _():
                        to_far(s, g, side).start()

    start = starts_ref[image]

    def coef(offset):
        total = jnp.float32(0.0)
        for k in range(4):
            total = total + jnp.where(start + k == image + offset, weights_ref[image, k], 0.0)
        return total

    coefs = [coef(offset) for offset in range(-2, 3)]

    def back(s, g, sender):
        return pltpu.make_async_remote_copy(
            src_ref=result.at[s, g],
            dst_ref=out_ref.at[0, s, pl.ds(sender * rows, rows)],
            send_sem=back_send.at[s, g],
            recv_sem=back_recv.at[s, sender],
            device_id={"gz": g},
            device_id_type=MESH,
        )

    def keep(s, g):
        return pltpu.make_async_copy(
            result.at[s, g], out_ref.at[0, s, pl.ds(gz * rows, rows)], back_send.at[s, g]
        )

    for s in both:
        for g in range(nz):
            for side in both:

                @pl.when(has_far[side])
                def _(s=s, g=g, side=side):
                    to_far(s, g, side).wait_recv()

            total = coefs[0] * far[0, s, g] + coefs[1] * near[0, s, g]
            total = total + coefs[2] * evolved[s, g]
            total = total + coefs[3] * near[1, s, g] + coefs[4] * far[1, s, g]
            result[s, g] = total

            @pl.when(gz != g)
            def _(s=s, g=g):
                back(s, g, gz).start()

            @pl.when(gz == g)
            def _(s=s, g=g):
                keep(s, g).start()

    for which in both:
        for k in range(nz):

            @pl.when(gz != k)
            def _(which=which, k=k):
                swap(which, k, gz).wait_send()

        @pl.when(gx < nx - 1)
        def _(which=which):
            edge_up(which, gz).wait_send()

        @pl.when(gx > 0)
        def _(which=which):
            edge_down(which, gz).wait_send()

    for step in range(1, STEPS):
        for s in both:

            @pl.when(strip < strips - 1)
            def _(s=s, step=step):
                row_up(step, s).wait_send()

            @pl.when(strip > 0)
            def _(s=s, step=step):
                row_down(step, s).wait_send()

    for s in both:
        for g in range(nz):
            for side in both:

                @pl.when(can_send[side])
                def _(s=s, g=g, side=side):
                    to_near(s, g, side).wait_send()

                @pl.when(can_send[side] & has_near[side])
                def _(s=s, g=g, side=side):
                    to_far(s, g, side).wait_send()

            @pl.when(gz != g)
            def _(s=s, g=g):
                back(s, g, gz).wait_send()
                back(s, g, g).wait_recv()

            @pl.when(gz == g)
            def _(s=s, g=g):
                keep(s, g).wait()


def local(sizes, species, diffusion, z_inverse, starts, weights):
    images, nx, nz, width, ny, lanes = sizes
    rows = width // nz
    depth = nz * lanes
    full = rows + 2 * HALO
    dma = pltpu.SemaphoreType.DMA
    anywhere = pl.BlockSpec(memory_space=pl.ANY)
    scalars = pl.BlockSpec(memory_space=pltpu.SMEM)
    lines = (2, nz, rows, ny, lanes)
    return pl.pallas_call(
        functools.partial(kernel, sizes),
        out_shape=jax.ShapeDtypeStruct(species.shape, jnp.float32),
        in_specs=[anywhere, anywhere, anywhere, scalars, scalars],
        out_specs=anywhere,
        scratch_shapes=[
            pltpu.VMEM((2, depth, depth), jnp.float32),
            pltpu.VMEM((2, depth, depth), jnp.bfloat16),
            pltpu.VMEM((2, depth, depth), jnp.bfloat16),
            pltpu.VMEM((2, nz, full, ny, lanes), jnp.float32),
            pltpu.VMEM((STEPS, 2, nz, full, ny, lanes), jnp.float32),
            pltpu.VMEM((2, 2 * rows * ny, depth), jnp.bfloat16),
            pltpu.VMEM(lines, jnp.float32),
            pltpu.VMEM((2, *lines), jnp.float32),
            pltpu.VMEM((2, *lines), jnp.float32),
            pltpu.VMEM(lines, jnp.float32),
            dma((3,)),
            dma((2, nz)),
            dma((2, nz)),
            dma((2, 2)),
            dma((2, 2, nz)),
            dma((STEPS, 2, 2)),
            dma((STEPS, 2, 2)),
            dma((2, 2, nz)),
            dma((2, 2, nz)),
            dma((2, 2, nz)),
            dma((2, 2, nz)),
            dma((2, nz)),
            dma((2, nz)),
        ],
        compiler_params=pltpu.CompilerParams(
            collective_id=0, has_side_effects=True, vmem_limit_bytes=48 * 1024 * 1024
        ),
    )(species, diffusion, z_inverse, starts, weights)


def solution(mesh):
    images, nx, nz = (mesh.shape[axis] for axis in ("img", "gx", "gz"))

    def body(species, diffusion, z_inverse, starts, weights):
        sizes = (images, nx, nz, *species.shape[2:])
        return local(sizes, species, diffusion, z_inverse, starts, weights)

    return jax.shard_map(
        body,
        mesh=mesh,
        in_specs=(P("img", None, "gx", None, "gz"), P(None, "gx", None, "gz"), P(), P(), P()),
        out_specs=P("img", None, "gx", None, "gz"),
        check_vma=False,
    )
```

time: 203 us -> 46.6 us (0.23); the launches traced: 201 us -> 46.4 us
  blocking collectives: 59.2 us -> 0 us
  local copies, waits for them, and re-layouts: 50.2 us -> 5.53 us
  Pallas kernels: 0 us -> 40.8 us
  starting transfers between devices: 35.5 us -> 0 us
  waiting for transfers between devices: 20.4 us -> 0 us
  between operations: 17.8 us -> 0.01 us
  other arithmetic: 8.99 us -> 0 us
  matrix products: 8.52 us -> 0 us
    all_to_all x7 -> x0, blocking collectives: 59.2 us -> none  [the longest x4 33.9 us: local(): lax.all_to_all(source, 'gz', split_axis=2, concat_axis=3, tiled=True)]
    pallas_call x0 -> x1, Pallas kernels: none -> 40.8 us  [local(): pl.pallas_call(functools.partial(kernel, sizes), out_shape=jax.ShapeDtype...]
    ppermute x14 -> x0, starting transfers between devices: 32.1 us -> none  [the longest x5 15 us: with_halo(): lax.ppermute(tail, axis, [(i, (i + 1) % count) for i in range(ends)])]
    unnamed x18 -> x11, local copies, waits for them, and re-layouts: 26.4 us -> 5.53 us
    ppermute x14 -> x0, waiting for transfers between devices: 15 us -> none  [the longest x5 14.8 us: with_halo(): lax.ppermute(head, axis, [((i + 1) % count, i) for i in range(ends)])]
    all_to_all x13 -> x0, local copies, waits for them, and re-layouts: 14.1 us -> none  [the longest x5 7.99 us: local(): lax.all_to_all(solved, 'gz', split_axis=3, concat_axis=2, tiled=True)]
    dot_general x4 -> x0, matrix products: 8.52 us -> none  [local(): jnp.einsum('sij,sabj->sabi', z_inverse, lax.all_to_all(source, 'gz', spli...]
    dot_general x4 -> x0, local copies, waits for them, and re-layouts: 6.95 us -> none  [local(): jnp.einsum('sij,sabj->sabi', z_inverse, lax.all_to_all(source, 'gz', spli...]
  transfers between devices with their start and end apart: 15 -> 0, of which waited for: 8 -> 0; matrix products, arithmetic and copies ran while one was open for 2% -> 0% of each run, Pallas kernels for 0% -> 0%
where the time goes in v1:
time: 46.6 us; the launch traced here: 46.4 us
  Pallas kernels  40.8 us (88%)
  local copies, waits for them, and re-layouts  5.53 us (12%)
    pallas_call x1, Pallas kernels, local(): pl.pallas_call(functools.partial(kernel, sizes), out_shape=jax.ShapeDtype...  40.8 us
    unnamed x11, local copies, waits for them, and re-layouts  5.53 us

profile of v1, /device:TPU:0, one launch (start us, length us, event | category | flops | bytes accessed | tf_op | source)
XLA Modules:
  0.0 46.4 jit_solution(17349277204395761585)
XLA Ops:
  0.0 0.0 copy-start
  0.0 1.6 %copy-done = f32[2,512,512]{2,1,0:T(8,128)S(1)} copy-done((f32[2,512,512]{2,1,0:T(8,128)S(1)}, f32[2,512,512]{2,1,0:T(8,128)}, u32[]{:S(2)}) %copy-start) | copy-done | bytes 2097176
  1.6 0.0 copy-start.1
  1.6 0.9 %copy-done.1 = f32[1,2,16,16,128]{4,3,2,1,0:T(8,128)S(1)} copy-done((f32[1,2,16,16,128]{4,3,2,1,0:T(8,128)S(1)}, f32[1,2,16,16,128]{4,3,2,1,0:T(8,128)}, u32[]{:S(2)}) %copy-start.1) | copy-done | bytes 262168
  2.5 0.0 copy-start.2
  2.5 0.9 %copy-done.2 = f32[2,16,16,128]{3,2,1,0:T(8,128)S(1)} copy-done((f32[2,16,16,128]{3,2,1,0:T(8,128)S(1)}, f32[2,16,16,128]{3,2,1,0:T(8,128)}, u32[]{:S(2)}) %copy-start.2) | copy-done | bytes 262168
  3.5 0.0 copy-start.3
  3.5 0.7 %copy-done.3 = f32[4,4]{1,0:T(4,128)S(1)} copy-done((f32[4,4]{1,0:T(4,128)S(1)}, f32[4,4]{1,0:T(4,128)}, u32[]{:S(2)}) %copy-start.3) | copy-done | bytes 88
  4.2 0.0 copy-start.4
  4.2 0.7 %copy-done.4 = s32[4]{0:T(128)S(1)} copy-done((s32[4]{0:T(128)S(1)}, s32[4]{0:T(128)}, u32[]{:S(2)}) %copy-start.4) | copy-done | bytes 40
  4.8 40.8 %shard_map.55 = f32[1,2,16,16,128]{4,3,2,1,0:T(8,128)S(1)} custom-call(f32[1,2,16,16,128]{4,3,2,1,0:T(8,128)S(1)} %copy-done.1, f32[2,16,16,128]{3,2,1,0:T(8,128)S(1)} %copy-done.2, f32[2,512,512]{2,1,0:T(8,128)S(1)} %copy-done, s32[4]{0:T(128)S(1)} %copy-done.4, f32[4,4]{1,0:T(4,128)S(1)} %copy-done.3), custom_call_target="tpu_custom_call" | custom-call | tf_op jit(solution)/shard_map/pallas_call | solution.py:442
  45.7 0.7 %copy.7 = f32[1,2,16,16,128]{4,3,2,1,0:T(8,128)} copy(f32[1,2,16,16,128]{4,3,2,1,0:T(8,128)S(1)} %shard_map.55) | data formatting | bytes 524288
Async XLA Ops:
  0.0 1.6 %copy-start = (f32[2,512,512]{2,1,0:T(8,128)S(1)}, f32[2,512,512]{2,1,0:T(8,128)}, u32[]{:S(2)}) copy-start(f32[2,512,512]{2,1,0:T(8,128)} %z_ref.1) | copy-start | bytes 6291460
  1.6 0.9 %copy-start.1 = (f32[1,2,16,16,128]{4,3,2,1,0:T(8,128)S(1)}, f32[1,2,16,16,128]{4,3,2,1,0:T(8,128)}, u32[]{:S(2)}) copy-start(f32[1,2,16,16,128]{4,3,2,1,0:T(8,128)} %species_ref.1) | copy-start | bytes 786436
  2.5 0.9 %copy-start.2 = (f32[2,16,16,128]{3,2,1,0:T(8,128)S(1)}, f32[2,16,16,128]{3,2,1,0:T(8,128)}, u32[]{:S(2)}) copy-start(f32[2,16,16,128]{3,2,1,0:T(8,128)} %diffusion_ref.1) | copy-start | bytes 786436
  3.5 0.7 %copy-start.3 = (f32[4,4]{1,0:T(4,128)S(1)}, f32[4,4]{1,0:T(4,128)}, u32[]{:S(2)}) copy-start(f32[4,4]{1,0:T(4,128)} %weights_ref.1) | copy-start | bytes 196
  4.2 0.7 %copy-start.4 = (s32[4]{0:T(128)S(1)}, s32[4]{0:T(128)}, u32[]{:S(2)}) copy-start(s32[4]{0:T(128)} %starts_ref.1) | copy-start | bytes 52

commit v2 on v1

--- a/solution.py
+++ b/solution.py
@@ -8,7 +8,7 @@
 from jax.sharding import PartitionSpec as P
 
 STEPS = 4
-HALO = 1
+HALO = 2
 
 
 step_size = 0.05
@@ -21,8 +21,8 @@
     species_ref,
     diffusion_ref,
     z_ref,
-    starts_ref,
-    weights_ref,
+    starts_hbm,
+    weights_hbm,
     out_ref,
     z_raw,
     z_high,
@@ -34,6 +34,8 @@
     near,
     far,
     result,
+    starts_ref,
+    weights_ref,
     local_sem,
     swap_send,
     swap_recv,
@@ -54,9 +56,14 @@
     strip = gx * nz + gz
     strips = nx * nz
     full = rows + 2 * HALO
+    trades = tuple(step for step in range(1, STEPS) if step % HALO == 0)
 
     load_z = pltpu.make_async_copy(z_ref, z_raw, local_sem.at[0])
     load_z.start()
+    load_starts = pltpu.make_async_copy(starts_hbm, starts_ref, local_sem.at[3])
+    load_starts.start()
+    load_weights = pltpu.make_async_copy(weights_hbm, weights_ref, local_sem.at[4])
+    load_weights.start()
 
     barrier = pltpu.get_barrier_semaphore()
     for step in range(1, nz):
@@ -157,12 +164,12 @@
 
     @pl.when(strip == 0)
     def _():
-        for part in (coeffs, *[states.at[i] for i in range(STEPS)]):
+        for part in (coeffs, *[states.at[i] for i in (0, *trades)]):
             part[:, :, 0:HALO] = jnp.zeros((2, nz, HALO, ny, lanes), jnp.float32)
 
     @pl.when(strip == strips - 1)
     def _():
-        for part in (coeffs, *[states.at[i] for i in range(STEPS)]):
+        for part in (coeffs, *[states.at[i] for i in (0, *trades)]):
             part[:, :, rows + HALO : full] = jnp.zeros((2, nz, HALO, ny, lanes), jnp.float32)
 
     def clear(condition, part):
@@ -210,8 +217,8 @@
     def row_up(step, s):
         p = strip + 1
         return pltpu.make_async_remote_copy(
-            src_ref=states.at[step, s, :, rows],
-            dst_ref=states.at[step, s, :, 0],
+            src_ref=states.at[step, s, :, rows : rows + HALO],
+            dst_ref=states.at[step, s, :, 0:HALO],
             send_sem=row_send.at[step, s, 0],
             recv_sem=row_recv.at[step, s, 0],
             device_id={"gx": lax.div(p, nz), "gz": lax.rem(p, nz)},
@@ -221,19 +228,17 @@
     def row_down(step, s):
         p = strip - 1 + nz
         return pltpu.make_async_remote_copy(
-            src_ref=states.at[step, s, :, 1],
-            dst_ref=states.at[step, s, :, rows + 1],
+            src_ref=states.at[step, s, :, HALO : 2 * HALO],
+            dst_ref=states.at[step, s, :, rows + HALO : full],
             send_sem=row_send.at[step, s, 1],
             recv_sem=row_recv.at[step, s, 1],
             device_id={"gx": lax.div(p, nz) - 1, "gz": lax.rem(p, nz)},
             device_id_type=MESH,
         )
 
-    place = lax.broadcasted_iota(jnp.int32, (rows, ny, lanes), 1)
     arrived(1)
     arrived(0)
     half = 0.5 * step_size
-    cells = rows * ny
 
     def to_near(s, g, side):
         return pltpu.make_async_remote_copy(
@@ -261,7 +266,7 @@
 
     for step in range(STEPS):
         state = states.at[step]
-        if step > 0:
+        if step in trades:
             for s in both:
 
                 @pl.when(strip > 0)
@@ -272,15 +277,25 @@
                 def _(s=s):
                     row_down(step, s).wait_recv()
 
+        spare = HALO - 1 - step % HALO
+        if step == STEPS - 1:
+            spare = 0
+        count = rows + 2 * spare
+        low, cells = HALO - spare, count * ny
+        inner = slice(low, low + count)
+        outer = slice(low - 1, low + count + 1)
+        place = lax.broadcasted_iota(jnp.int32, (count, ny, lanes), 1)
+        row = lax.broadcasted_iota(jnp.int32, (count, ny, lanes), 0)
+        beyond = (strip == 0) & (row < spare) | (strip == strips - 1) & (row >= rows + spare)
         for g in range(nz):
-            first, second = state[0, g, 1 : rows + 1], state[1, g, 1 : rows + 1]
+            first, second = state[0, g, inner], state[1, g, inner]
             reactions = (
                 first - first * first * first - second + 0.2,
                 0.5 * (first - second),
             )
             for s in both:
-                c = state[s, g]
-                d = coeffs[s, g]
+                c = state[s, g, outer]
+                d = coeffs[s, g, outer]
                 across = (d[:-1] + d[1:]) * (c[1:] - c[:-1])
                 centre, spread = c[1:-1], d[1:-1]
                 last = place == ny - 1
@@ -290,6 +305,8 @@
                 before = jnp.where(place == 0, spread * centre, pltpu.roll(along, 1, 1))
                 flux = (across[1:] - across[:-1]) + (along - before)
                 source = centre + step_size * reactions[s] + half * flux
+                if spare > 0:
+                    source = jnp.where(beyond, 0.0, source)
                 source = source.reshape(cells, lanes)
                 high = source.astype(jnp.bfloat16)
                 part = slice(g * lanes, (g + 1) * lanes)
@@ -301,12 +318,12 @@
             small = jnp.dot(lhs[s, 0:cells], z_low[s], preferred_element_type=jnp.float32)
             solved = product[0:cells] + (product[cells : 2 * cells] + small)
             for g in range(nz):
-                block = solved[:, g * lanes : (g + 1) * lanes].reshape(rows, ny, lanes)
+                block = solved[:, g * lanes : (g + 1) * lanes].reshape(count, ny, lanes)
                 if step < STEPS - 1:
-                    states[step + 1, s, g, 1 : rows + 1] = block
+                    states[step + 1, s, g, inner] = block
                 else:
                     evolved[s, g] = block
-            if step < STEPS - 1:
+            if step + 1 in trades:
 
                 @pl.when(strip < strips - 1)
                 def _(s=s, step=step):
@@ -316,7 +333,7 @@
                 def _(s=s, step=step):
                     row_down(step + 1, s).start()
 
-            else:
+            elif step == STEPS - 1:
                 for g in range(nz):
                     for side in both:
 
@@ -336,6 +353,8 @@
                     def _():
                         to_far(s, g, side).start()
 
+    load_starts.wait()
+    load_weights.wait()
     start = starts_ref[image]
 
     def coef(offset):
@@ -397,7 +416,7 @@
         def _(which=which):
             edge_down(which, gz).wait_send()
 
-    for step in range(1, STEPS):
+    for step in trades:
         for s in both:
 
             @pl.when(strip < strips - 1)
@@ -437,12 +456,11 @@
     full = rows + 2 * HALO
     dma = pltpu.SemaphoreType.DMA
     anywhere = pl.BlockSpec(memory_space=pl.ANY)
-    scalars = pl.BlockSpec(memory_space=pltpu.SMEM)
     lines = (2, nz, rows, ny, lanes)
     return pl.pallas_call(
         functools.partial(kernel, sizes),
         out_shape=jax.ShapeDtypeStruct(species.shape, jnp.float32),
-        in_specs=[anywhere, anywhere, anywhere, scalars, scalars],
+        in_specs=[anywhere] * 5,
         out_specs=anywhere,
         scratch_shapes=[
             pltpu.VMEM((2, depth, depth), jnp.float32),
@@ -450,12 +468,14 @@
             pltpu.VMEM((2, depth, depth), jnp.bfloat16),
             pltpu.VMEM((2, nz, full, ny, lanes), jnp.float32),
             pltpu.VMEM((STEPS, 2, nz, full, ny, lanes), jnp.float32),
-            pltpu.VMEM((2, 2 * rows * ny, depth), jnp.bfloat16),
+            pltpu.VMEM((2, 2 * (full - 2) * ny, depth), jnp.bfloat16),
             pltpu.VMEM(lines, jnp.float32),
             pltpu.VMEM((2, *lines), jnp.float32),
             pltpu.VMEM((2, *lines), jnp.float32),
             pltpu.VMEM(lines, jnp.float32),
-            dma((3,)),
+            pltpu.SMEM((images,), jnp.int32),
+            pltpu.SMEM((images, 4), jnp.float32),
+            dma((5,)),
             dma((2, nz)),
             dma((2, nz)),
             dma((2, 2)),
@@ -470,7 +490,7 @@
             dma((2, nz)),
         ],
         compiler_params=pltpu.CompilerParams(
-            collective_id=0, has_side_effects=True, vmem_limit_bytes=48 * 1024 * 1024
+            collective_id=0, has_side_effects=True, vmem_limit_bytes=62 * 1024 * 1024
         ),
     )(species, diffusion, z_inverse, starts, weights)
 

time: 46.6 us -> 40.3 us (0.86)
  local copies, waits for them, and re-layouts: 5.53 us -> 1.67 us
  Pallas kernels: 40.8 us -> 38.5 us
    unnamed x11 -> x1, local copies, waits for them, and re-layouts: 5.53 us -> 1.67 us
    pallas_call x1, Pallas kernels: 40.8 us -> 38.5 us  [local(): pl.pallas_call(functools.partial(kernel, sizes), out_shape=jax.ShapeDtype...]
where the time goes in v2:
time: 40.3 us; the launch traced here: 40.1 us
  Pallas kernels  38.5 us (96%)
  local copies, waits for them, and re-layouts  1.67 us (4%)
    pallas_call x1, Pallas kernels, local(): pl.pallas_call(functools.partial(kernel, sizes), out_shape=jax.ShapeDtype...  38.5 us
    unnamed x1, local copies, waits for them, and re-layouts  1.67 us

profile of v2, /device:TPU:0, one launch (start us, length us, event | category | flops | bytes accessed | tf_op | source)
XLA Modules:
  0.0 40.1 jit_solution(3440610789474492624)
XLA Ops:
  0.0 38.5 %shard_map.55 = f32[1,2,16,16,128]{4,3,2,1,0:T(8,128)} custom-call(f32[1,2,16,16,128]{4,3,2,1,0:T(8,128)} %species_ref.1, f32[2,16,16,128]{3,2,1,0:T(8,128)} %diffusion_ref.1, f32[2,512,512]{2,1,0:T(8,128)} %z_ref.1, s32[4]{0:T(128)} %starts_hbm.1, f32[4,4]{1,0:T(4,128)} %weights_hbm.1), custom_call_target="tpu_custom_call" | custom-call | tf_op jit(solution)/shard_map/pallas_call | solution.py:460
  38.5 1.7 %copy.7 = f32[1,2,16,16,128]{4,3,2,1,0:T(8,128)} copy(f32[1,2,16,16,128]{4,3,2,1,0:T(8,128)} %shard_map.55) | data formatting | bytes 524288

commit v3 on v2

--- a/solution.py
+++ b/solution.py
@@ -39,6 +39,8 @@
     local_sem,
     swap_send,
     swap_recv,
+    relay_send,
+    relay_recv,
     edge_send,
     edge_recv,
     row_send,
@@ -116,6 +118,37 @@
             device_id_type=MESH,
         )
 
+    paired = images % 2 == 0 and nz % 2 == 0
+    mine = lax.rem(image, 2)
+
+    def crosses(k, sender):
+        return paired and k // (nz // 2) != sender // (nz // 2)
+
+    def cross(k, sender):
+        low, high = span(k)
+        first = low - (k * rows - HALO)
+        return pltpu.make_async_remote_copy(
+            src_ref=diffusion_ref.at[mine, low:high],
+            dst_ref=coeffs.at[mine, sender, first : first + high - low],
+            send_sem=swap_send.at[0, k],
+            recv_sem=swap_recv.at[0, sender],
+            device_id={"gz": k},
+            device_id_type=MESH,
+        )
+
+    def relay(k, sender, species):
+        low, high = span(k)
+        first = low - (k * rows - HALO)
+        part = coeffs.at[species, sender, first : first + high - low]
+        return pltpu.make_async_remote_copy(
+            src_ref=part,
+            dst_ref=part,
+            send_sem=relay_send.at[sender],
+            recv_sem=relay_recv.at[sender],
+            device_id={"img": image + 1 - 2 * mine},
+            device_id_type=MESH,
+        )
+
     def own(which, k):
         low, high = span(k)
         first = low - (k * rows - HALO)
@@ -145,13 +178,23 @@
             device_id_type=MESH,
         )
 
+    for me in range(nz):
+
+        @pl.when(gz == me)
+        def _(me=me):
+            for k in range(nz):
+                if crosses(k, me):
+                    cross(k, me).start()
+
     for which in (1, 0):
         for me in range(nz):
 
             @pl.when(gz == me)
             def _(which=which, me=me):
-                for step in range(1, nz):
-                    swap(which, (me + step) % nz, me).start()
+                others = [(me + step) % nz for step in range(1, nz)]
+                for k in sorted(others, key=lambda k: not crosses(k, me)):
+                    if which == 1 or not crosses(k, me):
+                        swap(which, k, me).start()
                 own(which, me).start()
 
         @pl.when(gx < nx - 1)
@@ -191,6 +234,15 @@
             z_high[s, :, part] = high
             z_low[s, :, part] = (turned - high.astype(jnp.float32)).astype(jnp.bfloat16)
 
+    for me in range(nz):
+
+        @pl.when(gz == me)
+        def _(me=me):
+            for sender in range(nz):
+                if crosses(me, sender):
+                    cross(me, sender).wait_recv()
+                    relay(me, sender, mine).start()
+
     def arrived(which):
         for me in range(nz):
 
@@ -198,7 +250,9 @@
             def _(me=me):
                 own(which, me).wait()
                 for sender in range(nz):
-                    if sender != me:
+                    if which == 0 and crosses(me, sender):
+                        relay(me, sender, 1 - mine).wait_recv()
+                    elif sender != me:
                         low, high = span(me)
                         first = low - (me * rows - HALO)
                         part = targets[which].at[:, sender, first : first + high - low]
@@ -259,6 +313,9 @@
             device_id={"img": image + 1 - 2 * side},
             device_id_type=MESH,
         )
+
+    turns = [lax.rem(gz + turn, nz) for turn in range(1, nz)]
+    order = [(s, g) for s in both for g in turns] + [(s, gz) for s in both]
 
     can_send = (image < images - 1, image > 0)
     has_near = (image > 0, image < images - 1)
@@ -334,24 +391,24 @@
                     row_down(step + 1, s).start()
 
             elif step == STEPS - 1:
-                for g in range(nz):
+                ready = order[: nz - 1] if s == 0 else order[nz - 1 :]
+                for t, g in ready:
                     for side in both:
 
                         @pl.when(can_send[side])
-                        def _(s=s, g=g, side=side):
-                            to_near(s, g, side).start()
-
-    for s in both:
-        for g in range(nz):
-            for side in both:
-
-                @pl.when(has_near[side])
-                def _(s=s, g=g, side=side):
-                    to_near(s, g, side).wait_recv()
-
-                    @pl.when(can_send[side])
-                    def _():
-                        to_far(s, g, side).start()
+                        def _(t=t, g=g, side=side):
+                            to_near(t, g, side).start()
+
+    for s, g in order:
+        for side in both:
+
+            @pl.when(has_near[side])
+            def _(s=s, g=g, side=side):
+                to_near(s, g, side).wait_recv()
+
+                @pl.when(can_send[side])
+                def _():
+                    to_far(s, g, side).start()
 
     load_starts.wait()
     load_weights.wait()
@@ -380,33 +437,33 @@
             result.at[s, g], out_ref.at[0, s, pl.ds(gz * rows, rows)], back_send.at[s, g]
         )
 
-    for s in both:
-        for g in range(nz):
-            for side in both:
-
-                @pl.when(has_far[side])
-                def _(s=s, g=g, side=side):
-                    to_far(s, g, side).wait_recv()
-
-            total = coefs[0] * far[0, s, g] + coefs[1] * near[0, s, g]
-            total = total + coefs[2] * evolved[s, g]
-            total = total + coefs[3] * near[1, s, g] + coefs[4] * far[1, s, g]
-            result[s, g] = total
-
-            @pl.when(gz != g)
-            def _(s=s, g=g):
-                back(s, g, gz).start()
-
-            @pl.when(gz == g)
-            def _(s=s, g=g):
-                keep(s, g).start()
+    for turn, (s, g) in enumerate(order):
+        for side in both:
+
+            @pl.when(has_far[side])
+            def _(s=s, g=g, side=side):
+                to_far(s, g, side).wait_recv()
+
+        total = coefs[0] * far[0, s, g] + coefs[1] * near[0, s, g]
+        total = total + coefs[2] * evolved[s, g]
+        total = total + coefs[3] * near[1, s, g] + coefs[4] * far[1, s, g]
+        result[s, g] = total
+        if turn < len(order) - 2:
+            back(s, g, gz).start()
+        else:
+            keep(s, g).start()
 
     for which in both:
-        for k in range(nz):
-
-            @pl.when(gz != k)
-            def _(which=which, k=k):
-                swap(which, k, gz).wait_send()
+        for me in range(nz):
+
+            @pl.when(gz == me)
+            def _(which=which, me=me):
+                for k in range(nz):
+                    if which == 0 and crosses(k, me):
+                        cross(k, me).wait_send()
+                        relay(me, k, mine).wait_send()
+                    elif k != me:
+                        swap(which, k, me).wait_send()
 
         @pl.when(gx < nx - 1)
         def _(which=which):
@@ -457,6 +514,8 @@
     dma = pltpu.SemaphoreType.DMA
     anywhere = pl.BlockSpec(memory_space=pl.ANY)
     lines = (2, nz, rows, ny, lanes)
+    operands = (species, diffusion, z_inverse, starts, weights)
+    operands = [pltpu.with_memory_space_constraint(each, pltpu.HBM) for each in operands]
     return pl.pallas_call(
         functools.partial(kernel, sizes),
         out_shape=jax.ShapeDtypeStruct(species.shape, jnp.float32),
@@ -478,6 +537,8 @@
             dma((5,)),
             dma((2, nz)),
             dma((2, nz)),
+            dma((nz,)),
+            dma((nz,)),
             dma((2, 2)),
             dma((2, 2, nz)),
             dma((STEPS, 2, 2)),
@@ -490,9 +551,9 @@
             dma((2, nz)),
         ],
         compiler_params=pltpu.CompilerParams(
-            collective_id=0, has_side_effects=True, vmem_limit_bytes=62 * 1024 * 1024
+            collective_id=0, has_side_effects=True, vmem_limit_bytes=40 * 1024 * 1024
         ),
-    )(species, diffusion, z_inverse, starts, weights)
+    )(*operands)
 
 
 def solution(mesh):

time: 40.3 us -> 36.8 us (0.913)
  Pallas kernels: 38.5 us -> 36 us
  local copies, waits for them, and re-layouts: 1.67 us -> 0.71 us
    pallas_call x1, Pallas kernels: 38.5 us -> 36 us  [local(): pl.pallas_call(functools.partial(kernel, sizes), out_shape=jax.ShapeDtype...]
    unnamed x1, local copies, waits for them, and re-layouts: 1.67 us -> 0.71 us
where the time goes in v3:
time: 36.8 us; the launch traced here: 36.7 us
  Pallas kernels  36 us (98%)
  local copies, waits for them, and re-layouts  0.71 us (2%)
    pallas_call x1, Pallas kernels, local(): pl.pallas_call(functools.partial(kernel, sizes), out_shape=jax.ShapeDtype...  36 us

profile of v3, /device:TPU:0, one launch (start us, length us, event | category | flops | bytes accessed | tf_op | source)
XLA Modules:
  0.0 36.7 jit_solution(16537705225354217205)
XLA Ops:
  0.0 36.0 %shard_map.55 = f32[1,2,16,16,128]{4,3,2,1,0:T(8,128)S(1)} custom-call(f32[1,2,16,16,128]{4,3,2,1,0:T(8,128)} %species_ref.1, f32[2,16,16,128]{3,2,1,0:T(8,128)} %diffusion_ref.1, f32[2,512,512]{2,1,0:T(8,128)} %z_ref.1, s32[4]{0:T(128)} %starts_hbm.1, f32[4,4]{1,0:T(4,128)} %weights_hbm.1), custom_call_target="tpu_custom_call" | custom-call | tf_op jit(solution)/shard_map/pallas_call | solution.py:519
  36.0 0.7 %copy.7 = f32[1,2,16,16,128]{4,3,2,1,0:T(8,128)} copy(f32[1,2,16,16,128]{4,3,2,1,0:T(8,128)S(1)} %shard_map.55) | data formatting | bytes 524288

commit v4 on v3

--- a/solution.py
+++ b/solution.py
@@ -178,6 +178,16 @@
             device_id_type=MESH,
         )
 
+    for which in (1, 0):
+
+        @pl.when(gx < nx - 1)
+        def _(which=which):
+            edge_up(which, gz).start()
+
+        @pl.when(gx > 0)
+        def _(which=which):
+            edge_down(which, gz).start()
+
     for me in range(nz):
 
         @pl.when(gz == me)
@@ -196,14 +206,6 @@
                     if which == 1 or not crosses(k, me):
                         swap(which, k, me).start()
                 own(which, me).start()
-
-        @pl.when(gx < nx - 1)
-        def _(which=which):
-            edge_up(which, gz).start()
-
-        @pl.when(gx > 0)
-        def _(which=which):
-            edge_down(which, gz).start()
 
     @pl.when(strip == 0)
     def _():

time: 36.8 us -> 36.8 us (level)
  no operation moved by 1% of the time
where the time goes in v4:
time: 36.8 us; the launch traced here: 36.7 us
  Pallas kernels  35.9 us (98%)
  local copies, waits for them, and re-layouts  0.71 us (2%)
    pallas_call x1, Pallas kernels, local(): pl.pallas_call(functools.partial(kernel, sizes), out_shape=jax.ShapeDtype...  35.9 us

profile of v4, /device:TPU:0, one launch (start us, length us, event | category | flops | bytes accessed | tf_op | source)
XLA Modules:
  0.0 36.7 jit_solution(18335427538353981746)
XLA Ops:
  0.0 35.9 %shard_map.55 = f32[1,2,16,16,128]{4,3,2,1,0:T(8,128)S(1)} custom-call(f32[1,2,16,16,128]{4,3,2,1,0:T(8,128)} %species_ref.1, f32[2,16,16,128]{3,2,1,0:T(8,128)} %diffusion_ref.1, f32[2,512,512]{2,1,0:T(8,128)} %z_ref.1, s32[4]{0:T(128)} %starts_hbm.1, f32[4,4]{1,0:T(4,128)} %weights_hbm.1), custom_call_target="tpu_custom_call" | custom-call | tf_op jit(solution)/shard_map/pallas_call | solution.py:521
  35.9 0.7 %copy.7 = f32[1,2,16,16,128]{4,3,2,1,0:T(8,128)} copy(f32[1,2,16,16,128]{4,3,2,1,0:T(8,128)S(1)} %shard_map.55) | data formatting | bytes 524288
